TPU v7x, 256 devices: a whole 4x4x8 slice. The times are simulated.
256 devices in a mesh: ctx: 16 (over y, x), head: 8 (over z), pipe: 2 (over core).
Axes of the slice: x: 4, y: 4, z: 8, core: 2. Of those that a mesh axis runs over, the one named last changes fastest.
Arguments:
- queries: bfloat16 [2, 2048, 8192], P('pipe', 'ctx', 'head'), may hold values from -6 to 6
- keys: bfloat16 [2, 2048, 8192], P('pipe', 'ctx', 'head'), may hold values from -6 to 6
- values: bfloat16 [2, 2048, 8192], P('pipe', 'ctx', 'head'), may hold values from -6 to 6
- gates: bfloat16 [2, 2048, 8192], P('pipe', 'ctx', 'head'), may hold values from -6 to 6
- log_decay: float32 [2, 2048, 64], P('pipe', 'ctx', 'head'), may hold values from -1 to 0
- segment_ids: int32 [2, 2048], P('pipe', 'ctx'), may hold values from 0 to 7, never falling along the last dimension, each value on 1 to 512 neighbouring positions
- norm_gain: float32 [2, 8192], P('pipe', 'head'), may hold values from 0.1 to 1.9
- out_weight: bfloat16 [2, 8192, 6144], P('pipe', 'head', 'ctx'), may hold values from -0.0625 to 0.0625
Outputs:
- handed: bfloat16 [2, 2048, 6144], P('pipe', 'ctx', 'head')
Inputs may be any that keep to these rules, and one draw needn't show every extreme that they name: `segment_ids`: along each section's tokens the ids never fall; a document has at most a quarter of 2048 tokens, and one has exactly that many.
All inputs are finite; a program needn't handle non-finite values.
Results may differ from a plain program's by a relative error of at most 0.02.
Values may be sent and summed in bfloat16 or wider, within the bound.
A program may use at most 64 MiB of HBM per device.

v0:
```python
import jax
import jax.numpy as jnp
from jax import lax
from jax.sharding import PartitionSpec as P

DH = 128
highest = lax.Precision.HIGHEST


def entering(shard, axis, combine, identity):
    count, index = (lax.axis_size(axis), lax.axis_index(axis))
    everything = jax.tree.map(
        lambda part, kind: lax.all_gather(part.astype(kind), axis),
        shard,
        (jnp.bfloat16, jnp.bfloat16, jnp.bfloat16),
    )
    start = jax.tree.map(
        lambda part, zero: jnp.broadcast_to(jnp.asarray(zero, part.dtype), part.shape),
        shard,
        identity,
    )

    def hop(k, before):
        reached = k < index
        new = combine(
            before, jax.tree.map(lambda part, own: part[k].astype(own.dtype), everything, shard)
        )
        return jax.tree.map(lambda a, b: jnp.where(reached, a, b), new, before)

    return lax.fori_loop(0, count, hop, start)


def from_behind(shard, axis, by):
    count = lax.axis_size(axis)
    return lax.ppermute(shard, axis, [(i, (i + by) % count) for i in range(count)])


def block_step(carried, pieces):
    kv_state, doc_id = carried
    query_rows, key_rows, value_rows, rate_rows, doc_rows = pieces
    length = doc_rows.shape[0]
    running = jnp.cumsum(rate_rows, axis=0)
    running_t = running.T
    causal = lax.broadcasted_iota(jnp.int32, (length, length), 0) >= lax.broadcasted_iota(
        jnp.int32, (length, length), 1
    )
    allowed = causal & (doc_rows[:, None] == doc_rows[None, :])
    log_gaps = running_t[:, :, None] - running_t[:, None, :]
    weights = jnp.where(allowed[None], jnp.exp(jnp.where(allowed[None], log_gaps, 0.0)), 0.0)
    scores = jnp.einsum("ihd,jhd->hij", query_rows, key_rows, preferred_element_type=jnp.float32)
    mixed = (scores * weights).astype(jnp.bfloat16)
    inside = jnp.einsum("hij,jhd->ihd", mixed, value_rows, preferred_element_type=jnp.float32)
    value_full = value_rows.astype(jnp.float32)
    reaches = jnp.exp(running) * (doc_rows == doc_id).astype(jnp.float32)[:, None]
    carried_part = jnp.einsum(
        "ihd,hde->ihe",
        query_rows.astype(jnp.float32) * reaches[:, :, None],
        kv_state,
        precision=highest,
    )
    final_doc = doc_rows[-1]
    retain = (doc_id == final_doc).astype(jnp.float32)
    fading = (
        jnp.exp(running[-1][None, :] - running)
        * (doc_rows == final_doc).astype(jnp.float32)[:, None]
    )
    fresh_part = jnp.einsum(
        "jhd,jhe->hde",
        key_rows.astype(jnp.float32) * fading[:, :, None],
        value_full,
        precision=highest,
    )
    new_state = retain * jnp.exp(running[-1])[:, None, None] * kv_state + fresh_part
    return ((new_state, final_doc), inside + carried_part)


def sweep(query3, key3, value3, rate_rows, doc_rows, start_state, start_doc):
    rows_here = doc_rows.shape[0]
    heads_here = query3.shape[1]
    block_len = min(512, rows_here)
    block_count = rows_here // block_len
    pieces = (
        query3.reshape(block_count, block_len, heads_here, DH),
        key3.reshape(block_count, block_len, heads_here, DH),
        value3.reshape(block_count, block_len, heads_here, DH),
        rate_rows.reshape(block_count, block_len, heads_here),
        doc_rows.reshape(block_count, block_len),
    )
    final_carry, attended = lax.scan(block_step, (start_state, start_doc), pieces)
    return (final_carry[0], attended.reshape(rows_here, heads_here, DH))


def combine_pair(earlier, later):
    rate_early, state_early, doc_early = earlier
    rate_late, state_late, doc_late = later
    linked = ((doc_early == doc_late) | (doc_early < 0) | (doc_late < 0)).astype(jnp.float32)
    merged = linked[0] * rate_late[:, None, None] * state_early + state_late
    return (rate_early * rate_late, merged, jnp.where(doc_late < 0, doc_early, doc_late))


def carry_in(shard_rates, shard_state, shard_doc):
    heads_here = shard_rates.shape[0]
    neutral = (
        jnp.ones((heads_here,), jnp.float32),
        jnp.zeros((heads_here, DH, DH), jnp.float32),
        jnp.full((1,), -1.0, jnp.float32),
    )
    prefix = entering((shard_rates, shard_state, shard_doc), "ctx", combine_pair, neutral)
    return (prefix[1], prefix[2])


def on_device(queries, keys, values, gates, log_decay, segment_ids, norm_gain, out_weight):
    rows_here = queries.shape[1]
    width = queries.shape[2]
    heads_here = width // DH
    query3 = queries[0].reshape(rows_here, heads_here, DH)
    key3 = keys[0].reshape(rows_here, heads_here, DH)
    value3 = values[0].reshape(rows_here, heads_here, DH)
    rate_rows = log_decay[0]
    doc_rows = segment_ids[0].astype(jnp.float32)
    running = jnp.cumsum(rate_rows, axis=0)
    shard_rates = jnp.exp(running[-1])
    shard_doc = doc_rows[-1:]
    fading = (
        jnp.exp(running[-1][None, :] - running)
        * (doc_rows == shard_doc[0]).astype(jnp.float32)[:, None]
    )
    shard_state = jnp.einsum(
        "jhd,jhe->hde",
        key3.astype(jnp.float32) * fading[:, :, None],
        value3.astype(jnp.float32),
        precision=highest,
    )
    incoming, incoming_doc = carry_in(shard_rates, shard_state, shard_doc)
    ignored, attended = sweep(query3, key3, value3, rate_rows, doc_rows, incoming, incoming_doc[0])
    scaling = lax.rsqrt(jnp.mean(attended * attended, axis=-1, keepdims=True) + 1e-06)
    normed = (
        (attended * scaling).reshape(rows_here, width)
        * norm_gain[0][None, :]
        * jax.nn.sigmoid(gates[0].astype(jnp.float32))
    ).astype(jnp.bfloat16)
    weight_here = out_weight[0]
    partial_value = jnp.dot(
        normed,
        lax.all_gather(weight_here, "ctx", axis=1, tiled=True),
        preferred_element_type=jnp.float32,
    )
    summed = lax.psum_scatter(
        partial_value.astype(jnp.bfloat16), "head", scatter_dimension=1, tiled=True
    )
    handed = from_behind(summed, "pipe", 1)
    return handed[None]


def solution(mesh):
    return jax.shard_map(
        on_device,
        mesh=mesh,
        in_specs=(
            P("pipe", "ctx", "head"),
            P("pipe", "ctx", "head"),
            P("pipe", "ctx", "head"),
            P("pipe", "ctx", "head"),
            P("pipe", "ctx", "head"),
            P("pipe", "ctx"),
            P("pipe", "head"),
            P("pipe", "head", "ctx"),
        ),
        out_specs=P("pipe", "ctx", "head"),
        check_vma=False,
    )
```

profile of v0, /device:TPU:1, one launch (start us, length us, event | category | flops | bytes accessed | tf_op | source)
XLA Modules:
  0.0 237.9 jit_solution(17835527506379368174)
XLA Ops:
  8.8 1.3 compare_convert_fusion.1
  10.2 1.1 copy.36
  12.3 1.1 convolution_convert_fusion
  15.0 1.3 dynamic-slice.1
  17.0 34.4 %all-reduce = bf16[16]{0:T(256)(128)(2,1)S(1)} all-reduce(bf16[16]{0:T(256)(128)(2,1)S(1)} %dynamic-update-slice), channel_id=1, replica_groups=mesh['ctx'=16,'head'=8,'pipe'=2] {'ctx'}, use_global_device_ids=true, to_apply=%add | all-reduce | flops 16 | bytes 64
  51.4 14.6 %all-gather.2 = bf16[16,1,8]{2,1,0:T(2,128)(2,1)S(1)} all-gather(bf16[1,1,8]{2,1,0:T(2,128)(2,1)S(1)} %get-tuple-element.212), channel_id=1, replica_groups=mesh['ctx'=16,'head'=8,'pipe'=2] {'ctx'}, dimensions={0}, use_global_device_ids=true | all-gather | bytes 272 | tf_op jit(solution)/shard_map/all_gather | solution.py:13
  67.1 7.1 %all-gather.6.cloned.1.call-done = bf16[128,128,128]{2,1,0:T(8,128)(2,1)} async-done(((bf16[8,128,128]{2,1,0:T(8,128)(2,1)}), bf16[128,128,128]{2,1,0:T(8,128)(2,1)}) %all-gather.6.cloned.1.call-update) | async-done | bytes 4194320 | tf_op jit(solution)/shard_map/all_gather | solution.py:13
  74.2 62.4 %while.10 = (s32[]{:T(128)}, f32[8,128,128]{2,1,0:T(8,128)S(1)}, f32[1]{0:T(128)}, s32[]{:T(128)}, bf16[16,1]{0,1:T(2,128)(2,1)S(1)}, /*index=5*/bf16[16,8]{1,0:...) while((s32[]{:T(128)}, f32[8,128,128]{2,1,0:T(8,128)S(1)}, ...), condition=%wide.region_2.3_spmd.clone, body=%wide.region_1.2_spmd.clone.sunk | while | flops 655388 | bytes 1310999 | solution.py:30
  76.3 1.1 fusion.44
  80.2 1.1 fusion.44
  84.1 1.1 fusion.44
  88.0 1.1 fusion.44
  91.9 1.1 fusion.44
  95.8 1.1 fusion.44
  99.7 1.1 fusion.44
  103.6 1.1 fusion.44
  123.1 1.1 fusion.44
  127.0 1.1 fusion.44
  136.8 1.3 convolution_bitcast_fusion.1
  138.9 41.3 %all-gather.8.cloned.1.call-done = bf16[1,1024,6144]{2,1,0:T(8,128)(2,1)} async-done(((bf16[1,1024,384]{2,1,0:T(8,128)(2,1)}), bf16[1,1024,6144]{2,1,0:T(8,128)(2,1)}) %all-gather.8.cloned.1.call-update) | async-done | bytes 12582928 | tf_op jit(solution)/shard_map/all_gather | solution.py:145
  180.1 7.6 %fusion.6 = bf16[128,6144]{1,0:T(8,128)(2,1)} fusion(bf16[1,1024,6144]{2,1,0:T(8,128)(2,1)} %all-gather.8.cloned.1.call-done, bf16[1,128,1024]{2,1,0:T(8,128)(2,1)S(1)} %copy-done, f32[128,1024]{1,0:T(8,128)S(1)} %copy.34, f32[1024]{0:T(1024)S(1)} %bitcast.81), kind=kOutput, calls=%fused_computation.9 | convolution fusion | flops 1612316672 | bytes 14946304 | tf_op jit(solution)/shard_map/dot_general | solution.py:143
  187.8 37.0 %reduce-scatter.2.cloned.1.call-done = bf16[128,768]{1,0:T(8,128)(2,1)} async-done(((bf16[128,6144]{1,0:T(8,128)(2,1)}), bf16[128,768]{1,0:T(8,128)(2,1)}) %reduce-scatter.2.cloned.1.call-update) | async-done | bytes 196624 | tf_op jit(solution)/shard_map/reduce_scatter | solution.py:148
  224.8 4.6 %collective-permute-start = (bf16[128,768]{1,0:T(8,128)(2,1)}, bf16[128,768]{1,0:T(8,128)(2,1)S(1)}, u32[]{:S(2)}, u32[]{:S(2)}) collective-permute-start(bf16[128,768]{1,0:T(8,128)(2,1)} %reduce-scatter.2.cloned.1.call-done), channel_id=1, source_target_pairs={{0,1},{1,0},{2,3},{3,2},{4,5},{5,4},{6,7},{7,6},{8,9},{9,8},{10,11... | collective-permute-start | bytes 589832 | tf_op jit(solution)/shard_map/ppermute | solution.py:35
  229.4 1.3 collective-permute-done
  (73 shorter events, 25.0 us)
Async XLA Ops:
  6.5 67.7 %all-gather.6.cloned.1.call-start = ((), (), s32[]{:S(2)}) async-start(), calls=%async_computation.2 | async-start | bytes 4456448 | tf_op jit(solution)/shard_map/all_gather | solution.py:13
  13.5 123.2 %copy-start.2 = (s32[1,128]{1,0:T(1,128)S(1)}, s32[1,128]{1,0:T(1,128)}, u32[]{:S(2)}) copy-start(s32[1,128]{1,0:T(1,128)} %param.15) | copy-start | bytes 1540
  13.5 166.6 %all-gather.8.cloned.1.call-start = ((), (), s32[]{:S(2)}) async-start(), calls=%async_computation.3 | async-start | bytes 13369344 | tf_op jit(solution)/shard_map/all_gather | solution.py:145
  14.2 210.5 %reduce-scatter.2.cloned.1.call-start = ((), (), s32[]{:S(2)}) async-start(), calls=%async_computation.1 | async-start | bytes 1769472 | tf_op jit(solution)/shard_map/reduce_scatter | solution.py:148
  136.6 43.5 %copy-start = (bf16[1,128,1024]{2,1,0:T(8,128)(2,1)S(1)}, bf16[1,128,1024]{2,1,0:T(8,128)(2,1)}, u32[]{:S(2)}) copy-start(bf16[1,128,1024]{2,1,0:T(8,128)(2,1)} %param.13) | copy-start | bytes 786436
  136.6 43.5 %copy-start.1 = (f32[1,1024]{1,0:T(1,128)S(1)}, f32[1,1024]{1,0:T(1,128)}, u32[]{:S(2)}) copy-start(f32[1,1024]{1,0:T(1,128)} %param.16) | copy-start | bytes 12292
  224.8 5.9 %collective-permute-start = (bf16[128,768]{1,0:T(8,128)(2,1)}, bf16[128,768]{1,0:T(8,128)(2,1)S(1)}, u32[]{:S(2)}, u32[]{:S(2)}) collective-permute-start(bf16[128,768]{1,0:T(8,128)(2,1)} %reduce-scatter.2.cloned.1.call-done), channel_id=1, source_target_pairs={{0,1},{1,0},{2,3},{3,2},{4,5},{5,4},{6,7},{7,6},{8,9},{9,8},{10,11... | collective-permute-start | bytes 589832 | tf_op jit(solution)/shard_map/ppermute | solution.py:35
Sparse Core Ops, SparseCore 0:
  13.6 60.5 all-gather.5
  76.6 103.4 all-gather.7
  187.9 36.8 reduce-scatter.1
where the time goes:
time: 239 us; the launch traced here: 238 us
  waiting for transfers between devices  87.4 us (37%)
  blocking collectives  48.9 us (20%)
  loops' own time  34.1 us (14%)
  other arithmetic  20.2 us (8%)
  local copies, waits for them, and re-layouts  18.2 us (8%)
  between operations  13.9 us (6%)
  matrix products  10.5 us (4%)
  starting transfers between devices  4.7 us (2%)
    all_gather x1, waiting for transfers between devices, on_device(): lax.all_gather(weight_here, 'ctx', axis=1, tiled=True)  41.3 us
    reduce_scatter x1, waiting for transfers between devices, on_device(): lax.psum_scatter(partial_value.astype(jnp.bfloat16), 'head', scatter_dime...  37 us
    unnamed x1, blocking collectives  34.4 us
    another operation x1, loops' own time, entering(): return lax.fori_loop(0, count, hop, start)  34.1 us
    select_n x16, other arithmetic, hop(): return jax.tree.map(lambda a, b: jnp.where(reached, a, b), new, before)  17.5 us
    all_gather x1, blocking collectives, entering(): lax.all_gather(part.astype(kind), axis)  14.6 us
    dynamic_slice x16, local copies, waits for them, and re-layouts, hop(): part[k].astype(own.dtype)  10.6 us
    dot_general x1, matrix products, on_device(): jnp.dot(normed, lax.all_gather(weight_here, 'ctx', axis=1, tiled=True), p...  7.63 us
  transfers between devices with their start and end apart: 4, of which 4 were waited for; matrix products, arithmetic and copies ran while one was open for 14% of the time, Pallas kernels for 0%

commit v1 on v0

--- a/solution.py
+++ b/solution.py
@@ -142,7 +142,10 @@
     weight_here = out_weight[0]
     partial_value = jnp.dot(
         normed,
-        lax.all_gather(weight_here, "ctx", axis=1, tiled=True),
+        jnp.concatenate(
+            lax.all_to_all(jnp.stack([weight_here] * lax.axis_size("ctx"), axis=0), "ctx", 0, 0),
+            axis=1,
+        ),
         preferred_element_type=jnp.float32,
     )
     summed = lax.psum_scatter(

time: 239 us -> 406 us (1.70)
  blocking collectives: 48.9 us -> 241 us
  waiting for transfers between devices: 87.4 us -> 54.6 us
  starting transfers between devices: 4.7 us -> 12.4 us
  loops' own time: 34.1 us -> 27.4 us
  local copies, waits for them, and re-layouts: 18.2 us -> 22.4 us
    unnamed x1, blocking collectives: 34.4 us -> 228 us
    all_gather x1 -> x0, waiting for transfers between devices: 41.3 us -> none  [on_device(): lax.all_gather(weight_here, 'ctx', axis=1, tiled=True)]
    reduce_scatter x1, waiting for transfers between devices: 37 us -> 53.2 us  [on_device(): lax.psum_scatter(partial_value.astype(jnp.bfloat16), 'head', scatter_dime...]
    all_to_all x0 -> x1, starting transfers between devices: none -> 7.77 us  [on_device(): lax.all_to_all(jnp.stack([weight_here] * lax.axis_size('ctx'), axis=0), '...]
    another operation x0 -> x2, local copies, waits for them, and re-layouts: none -> 7.54 us  [the longest x1 6.14 us: on_device(): jnp.stack([weight_here] * lax.axis_size('ctx'), axis=0)]
    all_gather x1, waiting for transfers between devices: 7.12 us -> 0.02 us  [entering(): lax.all_gather(part.astype(kind), axis)]
    another operation x1, loops' own time: 34.1 us -> 27.4 us  [entering(): return lax.fori_loop(0, count, hop, start)]
  transfers between devices with their start and end apart: 4 -> 4, of which waited for: 4 -> 2; matrix products, arithmetic and copies ran while one was open for 14% -> 9% of each run, Pallas kernels for 0% -> 0%
where the time goes in v1:
time: 406 us; the launch traced here: 405 us
  blocking collectives  241 us (59%)
  waiting for transfers between devices  54.6 us (13%)
  loops' own time  27.4 us (7%)
  local copies, waits for them, and re-layouts  22.4 us (6%)
  other arithmetic  20.5 us (5%)
  between operations  14.2 us (3%)
  matrix products  12.9 us (3%)
  starting transfers between devices  12.4 us (3%)
    unnamed x1, blocking collectives  228 us
    reduce_scatter x1, waiting for transfers between devices, on_device(): lax.psum_scatter(partial_value.astype(jnp.bfloat16), 'head', scatter_dime...  53.2 us
    another operation x1, loops' own time, entering(): return lax.fori_loop(0, count, hop, start)  27.4 us
    select_n x16, other arithmetic, hop(): return jax.tree.map(lambda a, b: jnp.where(reached, a, b), new, before)  17.5 us
    all_gather x1, blocking collectives, entering(): lax.all_gather(part.astype(kind), axis)  13 us
    dot_general x1, matrix products, on_device(): jnp.dot(normed, jnp.concatenate(lax.all_to_all(jnp.stack([weight_here] *...  10 us
    dynamic_slice x16, local copies, waits for them, and re-layouts, hop(): part[k].astype(own.dtype)  8.93 us
  transfers between devices with their start and end apart: 4, of which 2 were waited for; matrix products, arithmetic and copies ran while one was open for 9% of the time, Pallas kernels for 0%

profile of v1, /device:TPU:1, one launch (start us, length us, event | category | flops | bytes accessed | tf_op | source)
XLA Modules:
  0.0 405.1 jit_solution(7000052862834203248)
XLA Ops:
  7.8 1.3 compare_convert_fusion.1
  10.2 1.1 copy.54
  12.3 1.1 convolution_convert_fusion.1
  13.5 1.4 copy.51
  14.9 6.1 %stack.3 = bf16[16,1024,384]{1,2,0:T(8,128)(2,1)} broadcast(bf16[1024,384]{0,1:T(8,128)(2,1)S(1)} %copy.51), dimensions={1,2} | broadcast | bytes 13369344 | tf_op jit(solution)/shard_map/stack | solution.py:146
  21.1 7.8 %all-to-all-start = ((bf16[16,1024,384]{1,2,0:T(8,128)(2,1)}), bf16[16,1024,384]{1,2,0:T(8,128)(2,1)}, u32[]{:S(2)}, u32[]{:S(2)}) async-start(bf16[16,1024,384]{1,2,0:T(8,128)(2,1)} %stack.3), calls=%async_computation | async-start | bytes 25165824 | tf_op jit(solution)/shard_map/all_to_all | solution.py:146
  30.9 227.6 %all-reduce = bf16[16]{0:T(256)(128)(2,1)S(1)} all-reduce(bf16[16]{0:T(256)(128)(2,1)S(1)} %dynamic-update-slice), channel_id=1, replica_groups=mesh['ctx'=16,'head'=8,'pipe'=2] {'ctx'}, use_global_device_ids=true, to_apply=%add | all-reduce | flops 16 | bytes 64
  258.5 13.0 %all-gather.1 = bf16[16,1,8]{2,1,0:T(2,128)(2,1)S(1)} all-gather(bf16[1,1,8]{2,1,0:T(2,128)(2,1)S(1)} %get-tuple-element.219), channel_id=1, replica_groups=mesh['ctx'=16,'head'=8,'pipe'=2] {'ctx'}, dimensions={0}, use_global_device_ids=true | all-gather | bytes 272 | tf_op jit(solution)/shard_map/all_gather | solution.py:13
  272.1 54.1 %while.10 = (s32[]{:T(128)}, f32[8,128,128]{2,1,0:T(8,128)S(1)}, f32[1]{0:T(128)}, s32[]{:T(128)}, bf16[16,1]{0,1:T(2,128)(2,1)S(1)}, /*index=5*/bf16[16,8]{1,0:...) while((s32[]{:T(128)}, f32[8,128,128]{2,1,0:T(8,128)S(1)}, ...), condition=%wide.region_2.3_spmd.clone, body=%wide.region_1.2_spmd.clone.sunk | while | flops 655388 | bytes 1311015 | solution.py:30
  287.9 1.1 fusion.36
  291.2 1.1 fusion.36
  294.6 1.1 fusion.36
  298.0 1.1 fusion.36
  301.4 1.1 fusion.36
  304.8 1.1 fusion.36
  308.2 1.1 fusion.36
  311.5 1.1 fusion.36
  314.9 1.1 fusion.36
  318.3 1.1 fusion.36
  326.3 1.3 convolution_bitcast_fusion.1
  328.3 10.0 %convolution_convert_fusion = bf16[128,6144]{1,0:T(8,128)(2,1)} fusion(bf16[128,1024]{0,1:T(8,128)(2,1)S(1)} %bitcast.65, bf16[1024,6144]{0,1:T(8,128)(2,1)} %bitcast.20), kind=kOutput, calls=%fused_computation.7 | convolution fusion | flops 1611399168 | bytes 14417920 | tf_op jit(solution)/shard_map/dot_general | solution.py:143
  338.4 53.2 %reduce-scatter.2.cloned.1.call-done = bf16[128,768]{1,0:T(8,128)(2,1)} async-done(((bf16[128,6144]{1,0:T(8,128)(2,1)}), bf16[128,768]{1,0:T(8,128)(2,1)}) %reduce-scatter.2.cloned.1.call-update) | async-done | bytes 196624 | tf_op jit(solution)/shard_map/reduce_scatter | solution.py:151
  391.7 4.6 %collective-permute-start = (bf16[128,768]{1,0:T(8,128)(2,1)}, bf16[128,768]{1,0:T(8,128)(2,1)S(1)}, u32[]{:S(2)}, u32[]{:S(2)}) collective-permute-start(bf16[128,768]{1,0:T(8,128)(2,1)} %reduce-scatter.2.cloned.1.call-done), channel_id=1, source_target_pairs={{0,1},{1,0},{2,3},{3,2},{4,5},{5,4},{6,7},{7,6},{8,9},{9,8},{10,11... | collective-permute-start | bytes 589832 | tf_op jit(solution)/shard_map/ppermute | solution.py:35
  396.3 1.3 collective-permute-done
  (79 shorter events, 22.6 us)
Async XLA Ops:
  6.5 265.5 %all-gather.4.cloned.1.call-start = ((), (), s32[]{:S(2)}) async-start(), calls=%async_computation.3 | async-start | bytes 4456448 | tf_op jit(solution)/shard_map/all_gather | solution.py:13
  21.0 8.5 %copy-start.4 = (u32[256]{0:T(256)S(1)}, u32[256]{0:T(256)}, u32[]{:S(2)}) copy-start(u32[256]{0:T(256)} %constant.78) | copy-start | bytes 3076
  21.0 250.5 %copy-start.1 = (bf16[1,128,1024]{2,1,0:T(8,128)(2,1)S(1)}, bf16[1,128,1024]{2,1,0:T(8,128)(2,1)}, u32[]{:S(2)}) copy-start(bf16[1,128,1024]{2,1,0:T(8,128)(2,1)} %param.10) | copy-start | bytes 786436
  21.0 250.5 %copy-start = (bf16[1,128,1024]{2,1,0:T(8,128)(2,1)S(1)}, bf16[1,128,1024]{2,1,0:T(8,128)(2,1)}, u32[]{:S(2)}) copy-start(bf16[1,128,1024]{2,1,0:T(8,128)(2,1)} %param.13) | copy-start | bytes 786436
  21.0 305.1 %copy-start.3 = (s32[1,128]{1,0:T(1,128)S(1)}, s32[1,128]{1,0:T(1,128)}, u32[]{:S(2)}) copy-start(s32[1,128]{1,0:T(1,128)} %param.15) | copy-start | bytes 1540
  21.1 307.3 %all-to-all-start = ((bf16[16,1024,384]{1,2,0:T(8,128)(2,1)}), bf16[16,1024,384]{1,2,0:T(8,128)(2,1)}, u32[]{:S(2)}, u32[]{:S(2)}) async-start(bf16[16,1024,384]{1,2,0:T(8,128)(2,1)} %stack.3), calls=%async_computation | async-start | bytes 25165824 | tf_op jit(solution)/shard_map/all_to_all | solution.py:146
  28.8 299.3 %copy-start.2 = (f32[1,1024]{1,0:T(1,128)S(1)}, f32[1,1024]{1,0:T(1,128)}, u32[]{:S(2)}) copy-start(f32[1,1024]{1,0:T(1,128)} %param.16) | copy-start | bytes 12292
  28.8 362.8 %reduce-scatter.2.cloned.1.call-start = ((), (), s32[]{:S(2)}) async-start(), calls=%async_computation.2 | async-start | bytes 1769472 | tf_op jit(solution)/shard_map/reduce_scatter | solution.py:151
  391.7 5.9 %collective-permute-start = (bf16[128,768]{1,0:T(8,128)(2,1)}, bf16[128,768]{1,0:T(8,128)(2,1)S(1)}, u32[]{:S(2)}, u32[]{:S(2)}) collective-permute-start(bf16[128,768]{1,0:T(8,128)(2,1)} %reduce-scatter.2.cloned.1.call-done), channel_id=1, source_target_pairs={{0,1},{1,0},{2,3},{3,2},{4,5},{5,4},{6,7},{7,6},{8,9},{9,8},{10,11... | collective-permute-start | bytes 589832 | tf_op jit(solution)/shard_map/ppermute | solution.py:35
Sparse Core Ops, SparseCore 0:
  13.6 215.2 all-gather.3
  338.5 53.0 reduce-scatter.1
